TPU v7x, 256 devices: a whole 4x4x8 slice. The times are simulated.
256 devices in a mesh: outer: 16 (over z, y_lo), dev: 16 (over x, y_hi, core).
Axes of the slice: x: 4, y: 4 (y_hi: 2, y_lo: 2; y = y_hi * 2 + y_lo), z: 8, core: 2. Of those that a mesh axis runs over, the one named last changes fastest.
Arguments:
- partials: bfloat16 [256, 8192, 256], P(('outer', 'dev')), may hold values from -6 to 6
- p_old: bfloat16 [8192, 1024], P('dev'), may hold values from -0.0625 to 0.0625
- p_new: bfloat16 [8192, 1024], P('dev'), may hold values from -0.0625 to 0.0625
- weight: float32 [8192, 256], P('dev'), may hold values from -4 to 4
- m_old: float32 [1024, 256], P('dev'), may hold values from -96 to 96
- v_old: float32 [1024, 256], P('dev'), may hold values from 32 to 1280
Outputs:
- new_weight: float32 [8192, 256], P('dev')
- m_new: float32 [1024, 256], P('dev')
- v_new: float32 [1024, 256], P('dev')
All inputs are finite; a program needn't handle non-finite values.
Results may differ from a plain program's by a relative error of at most 0.0012.
Values may be sent and summed in bfloat16 or wider, within the bound.
No kernel may reach another device: no remote copies, remote signals or barrier semaphores. Data moves between devices by JAX's collectives and lax.ppermute only.
A program may use at most 128 MiB of HBM per device.

v0:
```python
import jax
import jax.numpy as jnp
from jax import lax
from jax.sharding import PartitionSpec as P

beta_mean = 0.9
beta_square = 0.95
bias_mean = 0.9999734386011124
bias_square = 0.9940794707796659
adam_epsilon = 1e-08
step_scale = 0.5


def on_device(partials, p_old, p_new, weight, m_old, v_old):
    local_grad = partials[0].astype(jnp.float32)
    grad_cols = lax.psum_scatter(local_grad, "dev", scatter_dimension=1, tiled=True)
    proj_cols = jnp.dot(
        lax.all_gather(p_new, "dev", axis=0, tiled=True).astype(jnp.float32).T,
        grad_cols,
        precision=lax.Precision.HIGHEST,
    )
    proj_cols = lax.psum(proj_cols, "outer")
    projected = lax.all_to_all(proj_cols, "dev", split_axis=0, concat_axis=1, tiled=True)
    columns = p_new
    margin_rows = lax.psum_scatter(
        jnp.dot(columns.T, p_old, preferred_element_type=jnp.float32),
        "dev",
        scatter_dimension=0,
        tiled=True,
    )
    first_piece = lax.all_gather(m_old, "dev", axis=0, tiled=True)
    second_piece = lax.all_gather(v_old, "dev", axis=0, tiled=True)
    first = jnp.dot(margin_rows, first_piece, precision=lax.Precision.HIGHEST)
    second = jnp.dot(margin_rows * margin_rows, second_piece, precision=lax.Precision.HIGHEST)
    m_new = beta_mean * first + (1.0 - beta_mean) * projected
    v_new = beta_square * second + (1.0 - beta_square) * projected * projected
    direction = (m_new / bias_mean / (jnp.sqrt(v_new / bias_square) + adam_epsilon)).astype(
        jnp.bfloat16
    )
    columns = p_new
    update = jnp.dot(
        columns,
        lax.all_gather(direction, "dev", axis=0, tiled=True),
        preferred_element_type=jnp.float32,
    )
    new_weight = weight - step_scale * update
    return (new_weight, m_new, v_new)


def solution(mesh):
    in_specs = (
        P(("outer", "dev"), None, None),
        P("dev", None),
        P("dev", None),
        P("dev", None),
        P("dev", None),
        P("dev", None),
    )
    out_specs = (P("dev", None), P("dev", None), P("dev", None))
    return jax.shard_map(
        on_device, mesh=mesh, in_specs=in_specs, out_specs=out_specs, check_vma=False
    )
```

profile of v0, /device:TPU:1, one launch (start us, length us, event | category | flops | bytes accessed | tf_op | source)
XLA Modules:
  0.0 627.6 jit_solution(10560370040956481151)
XLA Ops:
  7.2 0.0 copy-start
  7.2 0.0 reduce-scatter.7.cloned.1.call-start
  7.2 6.2 bitcast_convert_fusion
  13.4 8.9 %copy.24 = f32[8192,256]{0,1:T(8,128)} copy(f32[8192,256]{1,0:T(8,128)} %bitcast_convert_fusion) | data formatting | bytes 16777216
  22.3 0.0 reduce-scatter.7.cloned.1.call-update
  22.3 0.0 all-gather.6.cloned.1.call-start
  22.4 0.7 all-gather.6.cloned.1.call-update
  23.1 0.0 copy-start.1
  23.1 0.0 all-reduce.2.cloned.1.call-start
  23.1 112.1 %reduce-scatter.7.cloned.1.call-done = f32[16,8192]{1,0:T(8,128)} async-done(((f32[256,8192]{1,0:T(8,128)}), f32[16,8192]{1,0:T(8,128)}) %reduce-scatter.7.cloned.1.call-update) | async-done | bytes 524304
  135.2 118.6 %all-gather.6.cloned.1.call-done = bf16[8192,1024]{1,0:T(8,128)(2,1)} async-done(((bf16[512,1024]{1,0:T(8,128)(2,1)}), bf16[8192,1024]{1,0:T(8,128)(2,1)}) %all-gather.6.cloned.1.call-update) | async-done | bytes 16777232 | tf_op jit(solution)/shard_map/all_gather | solution.py:18
  253.8 10.2 %fusion.4 = f32[1024,16]{0,1:T(8,128)S(1)} fusion(bf16[8192,1024]{1,0:T(8,128)(2,1)} %all-gather.6.cloned.1.call-done, f32[16,8192]{1,0:T(8,128)} %reduce-scatter.7.cloned.1.call-done), kind=kOutput, calls=%fused_computation.8 | convolution fusion | flops 1610612736 | bytes 17367040 | tf_op jit(solution)/shard_map/dot_general | solution.py:17
  264.1 0.0 copy-start.2
  264.1 0.1 all_to_all.14
  264.1 0.7 copy.18
  264.9 0.0 all-reduce.2.cloned.1.call-update
  264.9 0.0 all-gather.4.cloned.1.call-start
  264.9 0.5 all-gather.4.cloned.1.call-update
  265.5 0.0 reduce-scatter.5.cloned.1.call-start
  265.5 0.0 copy-done
  265.5 0.0 copy-done.1
  265.5 3.2 fusion.7
  268.8 0.0 reduce-scatter.5.cloned.1.call-update
  268.8 0.0 all-gather.8.cloned.1.call-start
  268.8 0.5 all-gather.8.cloned.1.call-update
  269.4 118.0 %all-reduce.2.cloned.1.call-done = f32[16,64,16]{1,2,0:T(8,128)} async-done(((f32[16,64,16]{1,2,0:T(8,128)}), f32[16,64,16]{1,2,0:T(8,128)}) %all-reduce.2.cloned.1.call-update) | async-done | bytes 65552 | tf_op jit(solution)/shard_map/psum | solution.py:22
  387.4 1.7 reshape.14
  389.0 17.0 %all-to-all-start = ((f32[16,1,1024]{2,1,0:T(1,128)}), f32[16,1,1024]{2,1,0:T(1,128)S(1)}, u32[]{:S(2)}, u32[]{:S(2)}) async-start(f32[16,1,1024]{2,1,0:T(1,128)} %reshape.14), calls=%async_computation.1 | async-start | bytes 131072 | tf_op jit(solution)/shard_map/all_to_all | solution.py:23
  406.0 0.0 copy-done.2
  406.0 0.2 copy.22
  406.2 7.2 %all-to-all-done = f32[16,1,1024]{2,1,0:T(1,128)S(1)} async-done(((f32[16,1,1024]{2,1,0:T(1,128)}), f32[16,1,1024]{2,1,0:T(1,128)S(1)}, u32[]{:S(2)}, u32[]{:S(2)}) %all-to-all-start) | async-done | bytes 65568 | tf_op jit(solution)/shard_map/all_to_all | solution.py:23
  413.4 0.5 broadcast.4
  413.9 0.8 reduce
  414.7 0.1 reshape.15
  414.8 0.1 copy.19
  414.9 35.6 %all-gather.4.cloned.1.call-done = f32[1024,256]{1,0:T(8,128)} async-done(((f32[64,256]{1,0:T(8,128)}), f32[1024,256]{1,0:T(8,128)}) %all-gather.4.cloned.1.call-update) | async-done | bytes 1048592 | tf_op jit(solution)/shard_map/all_gather | solution.py:31
  450.5 89.9 %reduce-scatter.5.cloned.1.call-done = f32[64,1024]{1,0:T(8,128)} async-done(((f32[1024,1024]{1,0:T(8,128)}), f32[64,1024]{1,0:T(8,128)}) %reduce-scatter.5.cloned.1.call-update) | async-done | bytes 262160 | tf_op jit(solution)/shard_map/reduce_scatter | solution.py:25
  540.3 1.9 fusion.3
  542.3 0.0 copy-start.3
  542.3 51.5 %all-gather.8.cloned.1.call-done = f32[1024,256]{1,0:T(8,128)} async-done(((f32[64,256]{1,0:T(8,128)}), f32[1024,256]{1,0:T(8,128)}) %all-gather.8.cloned.1.call-update) | async-done | bytes 1048592 | tf_op jit(solution)/shard_map/all_gather | solution.py:32
  593.8 2.6 divide_convert_fusion
  596.4 22.9 %all_gather.15 = bf16[1024,256]{1,0:T(8,128)(2,1)S(1)} all-gather(bf16[64,256]{1,0:T(8,128)(2,1)S(1)} %get-tuple-element.12), channel_id=1, replica_groups=mesh['outer'=16,'dev'=16] {'dev'}, dimensions={0}, use_global_device_ids=true | all-gather | bytes 557056 | tf_op jit(solution)/shard_map/all_gather | solution.py:43
  619.3 0.5 fusion.1
  619.8 1.0 copy.23
  620.8 0.0 copy-done.3
Async XLA Ops:
  7.2 258.3 %copy-start = (bf16[512,1024]{1,0:T(8,128)(2,1)S(1)}, bf16[512,1024]{1,0:T(8,128)(2,1)}, u32[]{:S(2)}) copy-start(bf16[512,1024]{1,0:T(8,128)(2,1)} %param.7) | copy-start | bytes 3145732
  7.2 128.1 %reduce-scatter.7.cloned.1.call-start = ((), (), s32[]{:S(2)}) async-start(), calls=%async_computation.8 | async-start | bytes 8912896
  22.3 231.5 %all-gather.6.cloned.1.call-start = ((), (), s32[]{:S(2)}) async-start(), calls=%async_computation.5 | async-start | bytes 17825792 | tf_op jit(solution)/shard_map/all_gather | solution.py:18
  23.1 242.4 %copy-start.1 = (bf16[512,1024]{1,0:T(8,128)(2,1)S(1)}, bf16[512,1024]{1,0:T(8,128)(2,1)}, u32[]{:S(2)}) copy-start(bf16[512,1024]{1,0:T(8,128)(2,1)} %param.8) | copy-start | bytes 3145732
  23.1 364.3 %all-reduce.2.cloned.1.call-start = ((), (), s32[]{:S(2)}) async-start(), calls=%async_computation.6 | async-start | bytes 262144 | tf_op jit(solution)/shard_map/psum | solution.py:22
  264.1 142.0 %copy-start.2 = (f32[512,256]{1,0:T(8,128)S(1)}, f32[512,256]{1,0:T(8,128)}, u32[]{:S(2)}) copy-start(f32[512,256]{1,0:T(8,128)} %param.9) | copy-start | bytes 1572868
  264.9 185.6 %all-gather.4.cloned.1.call-start = ((), (), s32[]{:S(2)}) async-start(), calls=%async_computation.4 | async-start | bytes 1114112 | tf_op jit(solution)/shard_map/all_gather | solution.py:31
  265.5 274.9 %reduce-scatter.5.cloned.1.call-start = ((), (), s32[]{:S(2)}) async-start(), calls=%async_computation.3 | async-start | bytes 4456448 | tf_op jit(solution)/shard_map/reduce_scatter | solution.py:25
  268.8 325.0 %all-gather.8.cloned.1.call-start = ((), (), s32[]{:S(2)}) async-start(), calls=%async_computation.7 | async-start | bytes 1114112 | tf_op jit(solution)/shard_map/all_gather | solution.py:32
  389.0 24.4 %all-to-all-start = ((f32[16,1,1024]{2,1,0:T(1,128)}), f32[16,1,1024]{2,1,0:T(1,128)S(1)}, u32[]{:S(2)}, u32[]{:S(2)}) async-start(f32[16,1,1024]{2,1,0:T(1,128)} %reshape.14), calls=%async_computation.1 | async-start | bytes 131072 | tf_op jit(solution)/shard_map/all_to_all | solution.py:23
  542.3 78.5 %copy-start.3 = (f32[64,256]{1,0:T(8,128)}, f32[64,256]{1,0:T(8,128)S(1)}, u32[]{:S(2)}) copy-start(f32[64,256]{1,0:T(8,128)S(1)} %fusion.3) | copy-start | bytes 196612
Sparse Core Ops, SparseCore 0:
  22.5 112.7 reduce-scatter.6
  137.9 115.8 all-gather.5
  265.0 122.3 all-reduce.1
  390.3 60.1 all-gather.3
  455.3 85.0 reduce-scatter.4
  542.9 50.8 all-gather.7
where the time goes:
time: 628 us
  waiting for transfers between devices  535 us (85%)
  blocking collectives  22.9 us (4%)
  matrix products  18.5 us (3%)
  starting transfers between devices  17.2 us (3%)
  between operations  14.2 us (2%)
  local copies, waits for them, and re-layouts  13.3 us (2%)
  other arithmetic  6.96 us (1%)
    all_gather x1, waiting for transfers between devices, on_device(): lax.all_gather(p_new, 'dev', axis=0, tiled=True).astype(jnp.float32)  119 us
    psum x1, waiting for transfers between devices, on_device(): proj_cols = lax.psum(proj_cols, 'outer')  118 us
    unnamed x7, waiting for transfers between devices  114 us
    reduce_scatter x1, waiting for transfers between devices, on_device(): lax.psum_scatter(jnp.dot(columns.T, p_old, preferred_element_type=jnp.flo...  89.9 us
    all_gather x1, waiting for transfers between devices, on_device(): second_piece = lax.all_gather(v_old, 'dev', axis=0, tiled=True)  51.5 us
    all_gather x1, waiting for transfers between devices, on_device(): first_piece = lax.all_gather(m_old, 'dev', axis=0, tiled=True)  35.6 us
    all_gather x1, blocking collectives, on_device(): lax.all_gather(direction, 'dev', axis=0, tiled=True)  22.9 us
    all_to_all x1, starting transfers between devices, on_device(): lax.all_to_all(proj_cols, 'dev', split_axis=0, concat_axis=1, tiled=True)  17 us
  transfers between devices with their start and end apart: 7, of which 7 were waited for; matrix products, arithmetic and copies ran while one was open for 1% of the time, Pallas kernels for 0%

commit v1 on v0

--- a/solution.py
+++ b/solution.py
@@ -19,7 +19,7 @@
         grad_cols,
         precision=lax.Precision.HIGHEST,
     )
-    proj_cols = lax.psum(proj_cols, "outer")
+    proj_cols = jnp.sum(lax.all_gather(proj_cols, "outer"), axis=0)
     projected = lax.all_to_all(proj_cols, "dev", split_axis=0, concat_axis=1, tiled=True)
     columns = p_new
     margin_rows = lax.psum_scatter(

time: 628 us -> 562 us (0.89)
  waiting for transfers between devices: 535 us -> 467 us
    psum x1 -> x0, waiting for transfers between devices: 118 us -> none  [on_device(): proj_cols = lax.psum(proj_cols, 'outer')]
    all_gather x0 -> x1, waiting for transfers between devices: none -> 51.5 us  [on_device(): proj_cols = jnp.sum(lax.all_gather(proj_cols, 'outer'), axis=0)]
    unnamed x13 -> x14, local copies, waits for them, and re-layouts: 11.9 us -> 12.8 us
  transfers between devices with their start and end apart: 7 -> 7, of which waited for: 7 -> 7; matrix products, arithmetic and copies ran while one was open for 1% -> 2% of each run, Pallas kernels for 0% -> 0%
where the time goes in v1:
time: 562 us; the launch traced here: 561 us
  waiting for transfers between devices  467 us (83%)
  blocking collectives  22.9 us (4%)
  matrix products  19.1 us (3%)
  starting transfers between devices  17.7 us (3%)
  between operations  14.2 us (3%)
  local copies, waits for them, and re-layouts  13.5 us (2%)
  other arithmetic  7.11 us (1%)
    all_gather x1, waiting for transfers between devices, on_device(): lax.all_gather(p_new, 'dev', axis=0, tiled=True).astype(jnp.float32)  119 us
    unnamed x7, waiting for transfers between devices  114 us
    reduce_scatter x1, waiting for transfers between devices, on_device(): lax.psum_scatter(jnp.dot(columns.T, p_old, preferred_element_type=jnp.flo...  89.4 us
    all_gather x1, waiting for transfers between devices, on_device(): second_piece = lax.all_gather(v_old, 'dev', axis=0, tiled=True)  51.8 us
    all_gather x1, waiting for transfers between devices, on_device(): proj_cols = jnp.sum(lax.all_gather(proj_cols, 'outer'), axis=0)  51.5 us
    all_gather x1, waiting for transfers between devices, on_device(): first_piece = lax.all_gather(m_old, 'dev', axis=0, tiled=True)  34.7 us
    all_gather x1, blocking collectives, on_device(): lax.all_gather(direction, 'dev', axis=0, tiled=True)  22.9 us
    all_to_all x1, starting transfers between devices, on_device(): lax.all_to_all(proj_cols, 'dev', split_axis=0, concat_axis=1, tiled=True)  17.4 us
  transfers between devices with their start and end apart: 7, of which 7 were waited for; matrix products, arithmetic and copies ran while one was open for 2% of the time, Pallas kernels for 0%

profile of v1, /device:TPU:1, one launch (start us, length us, event | category | flops | bytes accessed | tf_op | source)
XLA Modules:
  0.0 561.5 jit_solution(1038839888395518812)
XLA Ops:
  7.2 0.0 copy-start
  7.2 0.0 reduce-scatter.7.cloned.1.call-start
  7.2 6.2 %bitcast_convert_fusion = f32[8192,256]{1,0:T(8,128)} fusion(bf16[1,8192,256]{2,1,0:T(8,128)(2,1)} %param.6), kind=kLoop, calls=%fused_computation | loop fusion | flops 2097152 | bytes 12582912 | tf_op jit(solution)/shard_map/convert_element_type | solution.py:15
  13.4 8.9 %copy.23 = f32[8192,256]{0,1:T(8,128)} copy(f32[8192,256]{1,0:T(8,128)} %bitcast_convert_fusion) | data formatting | bytes 16777216
  22.3 0.0 reduce-scatter.7.cloned.1.call-update
  22.3 0.0 all-gather.8.cloned.1.call-start
  22.4 0.7 all-gather.8.cloned.1.call-update
  23.1 0.0 copy-start.1
  23.1 0.0 all-gather.12.cloned.1.call-start
  23.1 112.1 %reduce-scatter.7.cloned.1.call-done = f32[16,8192]{1,0:T(8,128)} async-done(((f32[256,8192]{1,0:T(8,128)}), f32[16,8192]{1,0:T(8,128)}) %reduce-scatter.7.cloned.1.call-update) | async-done | bytes 524304
  135.2 118.6 %all-gather.8.cloned.1.call-done = bf16[8192,1024]{1,0:T(8,128)(2,1)} async-done(((bf16[512,1024]{1,0:T(8,128)(2,1)}), bf16[8192,1024]{1,0:T(8,128)(2,1)}) %all-gather.8.cloned.1.call-update) | async-done | bytes 16777232 | tf_op jit(solution)/shard_map/all_gather | solution.py:18
  253.8 10.8 %fusion.4 = f32[1024,16]{0,1:T(8,128)} fusion(bf16[8192,1024]{1,0:T(8,128)(2,1)} %all-gather.8.cloned.1.call-done, f32[16,8192]{1,0:T(8,128)} %reduce-scatter.7.cloned.1.call-done), kind=kOutput, calls=%fused_computation.9 | convolution fusion | flops 1610612736 | bytes 17367040 | tf_op jit(solution)/shard_map/dot_general | solution.py:17
  264.7 0.0 copy-start.2
  264.7 0.0 all-gather.12.cloned.1.call-update
  264.7 0.0 all-gather.6.cloned.1.call-start
  264.8 0.5 all-gather.6.cloned.1.call-update
  265.3 0.0 reduce-scatter.5.cloned.1.call-start
  265.3 0.0 copy-done
  265.3 0.0 copy-done.1
  265.4 3.2 fusion.7
  268.6 0.0 reduce-scatter.5.cloned.1.call-update
  268.6 0.0 all-gather.10.cloned.1.call-start
  268.7 0.5 all-gather.10.cloned.1.call-update
  269.2 51.5 %all-gather.12.cloned.1.call-done = f32[16384,16]{0,1:T(8,128)} async-done(((f32[1024,16]{0,1:T(8,128)}), f32[16384,16]{0,1:T(8,128)}) %all-gather.12.cloned.1.call-update) | async-done | bytes 1048592 | tf_op jit(solution)/shard_map/all_gather | solution.py:22
  320.7 1.8 copy.25
  322.5 0.2 bitcast_reduce_fusion
  322.7 0.1 all_to_all.14
  322.8 0.8 reshape.15
  323.6 17.4 %all-to-all-start = ((f32[16,1,1024]{2,1,0:T(1,128)}), f32[16,1,1024]{2,1,0:T(1,128)S(1)}, u32[]{:S(2)}, u32[]{:S(2)}) async-start(f32[16,1,1024]{2,1,0:T(1,128)} %reshape.15), calls=%async_computation.1 | async-start | bytes 131072 | tf_op jit(solution)/shard_map/all_to_all | solution.py:23
  341.0 0.0 copy-done.2
  341.0 0.2 copy.21
  341.2 7.2 %all-to-all-done = f32[16,1,1024]{2,1,0:T(1,128)S(1)} async-done(((f32[16,1,1024]{2,1,0:T(1,128)}), f32[16,1,1024]{2,1,0:T(1,128)S(1)}, u32[]{:S(2)}, u32[]{:S(2)}) %all-to-all-start) | async-done | bytes 65568 | tf_op jit(solution)/shard_map/all_to_all | solution.py:23
  348.4 0.5 broadcast.4
  348.9 0.8 reduce
  349.7 0.1 reshape.16
  349.8 0.1 copy.18
  349.9 34.7 %all-gather.6.cloned.1.call-done = f32[1024,256]{1,0:T(8,128)} async-done(((f32[64,256]{1,0:T(8,128)}), f32[1024,256]{1,0:T(8,128)}) %all-gather.6.cloned.1.call-update) | async-done | bytes 1048592 | tf_op jit(solution)/shard_map/all_gather | solution.py:31
  384.6 89.4 %reduce-scatter.5.cloned.1.call-done = f32[64,1024]{1,0:T(8,128)} async-done(((f32[1024,1024]{1,0:T(8,128)}), f32[64,1024]{1,0:T(8,128)}) %reduce-scatter.5.cloned.1.call-update) | async-done | bytes 262160 | tf_op jit(solution)/shard_map/reduce_scatter | solution.py:25
  473.9 1.9 fusion.3
  475.9 0.0 copy-start.3
  475.9 51.8 %all-gather.10.cloned.1.call-done = f32[1024,256]{1,0:T(8,128)} async-done(((f32[64,256]{1,0:T(8,128)}), f32[1024,256]{1,0:T(8,128)}) %all-gather.10.cloned.1.call-update) | async-done | bytes 1048592 | tf_op jit(solution)/shard_map/all_gather | solution.py:32
  527.6 2.6 divide_convert_fusion
  530.3 22.9 %all_gather.23 = bf16[1024,256]{1,0:T(8,128)(2,1)S(1)} all-gather(bf16[64,256]{1,0:T(8,128)(2,1)S(1)} %get-tuple-element.12), channel_id=1, replica_groups=mesh['outer'=16,'dev'=16] {'dev'}, dimensions={0}, use_global_device_ids=true | all-gather | bytes 557056 | tf_op jit(solution)/shard_map/all_gather | solution.py:43
  553.1 0.5 fusion.1
  553.6 1.0 copy.22
  554.6 0.0 copy-done.3
  (1 shorter events, 0.0 us)
Async XLA Ops:
  7.2 258.2 %copy-start = (bf16[512,1024]{1,0:T(8,128)(2,1)S(1)}, bf16[512,1024]{1,0:T(8,128)(2,1)}, u32[]{:S(2)}) copy-start(bf16[512,1024]{1,0:T(8,128)(2,1)} %param.7) | copy-start | bytes 3145732
  7.2 128.1 %reduce-scatter.7.cloned.1.call-start = ((), (), s32[]{:S(2)}) async-start(), calls=%async_computation.8 | async-start | bytes 8912896
  22.3 231.5 %all-gather.8.cloned.1.call-start = ((), (), s32[]{:S(2)}) async-start(), calls=%async_computation.5 | async-start | bytes 17825792 | tf_op jit(solution)/shard_map/all_gather | solution.py:18
  23.1 242.3 %copy-start.1 = (bf16[512,1024]{1,0:T(8,128)(2,1)S(1)}, bf16[512,1024]{1,0:T(8,128)(2,1)}, u32[]{:S(2)}) copy-start(bf16[512,1024]{1,0:T(8,128)(2,1)} %param.8) | copy-start | bytes 3145732
  23.1 297.6 %all-gather.12.cloned.1.call-start = ((), (), s32[]{:S(2)}) async-start(), calls=%async_computation.7 | async-start | bytes 1114112 | tf_op jit(solution)/shard_map/all_gather | solution.py:22
  264.7 76.3 %copy-start.2 = (f32[512,256]{1,0:T(8,128)S(1)}, f32[512,256]{1,0:T(8,128)}, u32[]{:S(2)}) copy-start(f32[512,256]{1,0:T(8,128)} %param.9) | copy-start | bytes 1572868
  264.7 119.9 %all-gather.6.cloned.1.call-start = ((), (), s32[]{:S(2)}) async-start(), calls=%async_computation.4 | async-start | bytes 1114112 | tf_op jit(solution)/shard_map/all_gather | solution.py:31
  265.3 208.6 %reduce-scatter.5.cloned.1.call-start = ((), (), s32[]{:S(2)}) async-start(), calls=%async_computation.3 | async-start | bytes 4456448 | tf_op jit(solution)/shard_map/reduce_scatter | solution.py:25
  268.6 259.0 %all-gather.10.cloned.1.call-start = ((), (), s32[]{:S(2)}) async-start(), calls=%async_computation.6 | async-start | bytes 1114112 | tf_op jit(solution)/shard_map/all_gather | solution.py:32
  323.6 24.8 %all-to-all-start = ((f32[16,1,1024]{2,1,0:T(1,128)}), f32[16,1,1024]{2,1,0:T(1,128)S(1)}, u32[]{:S(2)}, u32[]{:S(2)}) async-start(f32[16,1,1024]{2,1,0:T(1,128)} %reshape.15), calls=%async_computation.1 | async-start | bytes 131072 | tf_op jit(solution)/shard_map/all_to_all | solution.py:23
  475.9 78.8 %copy-start.3 = (f32[64,256]{1,0:T(8,128)}, f32[64,256]{1,0:T(8,128)S(1)}, u32[]{:S(2)}) copy-start(f32[64,256]{1,0:T(8,128)S(1)} %fusion.3) | copy-start | bytes 196612
Sparse Core Ops, SparseCore 0:
  22.5 112.7 reduce-scatter.6
  137.9 115.8 all-gather.7
  264.8 55.8 all-gather.11
  323.2 61.2 all-gather.5
  388.8 85.1 reduce-scatter.4
  476.8 50.7 all-gather.9
